TPU v7x, 128 devices: a whole 4x4x4 slice. The times are simulated.
128 devices in a mesh: chan: 16 (over y, x), tm: 8 (over z, core).
Axes of the slice: x: 4, y: 4, z: 4, core: 2. Of those that a mesh axis runs over, the one named last changes fastest.
Arguments:
- samples: bfloat16 [256, 192, 4096], P('chan', 'tm'), may hold values from -6 to 6
- taps: float32 [16, 4096], replicated, may hold values from -1.5 to 1.5
- block_tile: int32 [120], replicated, may hold values from 0 to 15, as said below
- tile_slots: int32 [16], replicated, may hold values from 0 to 15, as said below
- kern_u: bfloat16 [16, 30720], replicated, may hold values from -1.1953125 to 1.1953125
- kern_v: bfloat16 [16, 30720], replicated, may hold values from -1.1953125 to 1.1953125
Outputs:
- uv_grid: float32 [16, 2048, 2, 256], P('tm', 'chan')
Inputs may be any that keep to these rules, and one draw needn't show every extreme that they name: `block_tile`: A tile's owner is (its position in tile_slots) // 2. The blocks that fall in the tiles of one owner are at most 30; in every draw one owner has exactly 30. `tile_slots`: each tile number stands once.
All inputs are finite; a program needn't handle non-finite values.
Results may differ from a plain program's by a relative error of at most 0.0077.
Values may be sent and summed in bfloat16 or wider, within the bound.
No kernel may reach another device: no remote copies, remote signals or barrier semaphores. Data moves between devices by JAX's collectives and lax.ppermute only.
A program may use at most 192 MiB of HBM per device.

v0:
```python
import math
import jax
import jax.numpy as jnp
import numpy as np
from jax import lax
from jax.sharding import PartitionSpec as P

SBLK = 16
GRID = 16


def passed_along(value, axis, steps):
    count = lax.axis_size(axis)
    leading, last = (max(0, -steps), min(count, count - steps))
    return lax.ppermute(value, axis, [(source, source + steps) for source in range(leading, last)])


def block_pairs(block_total):
    left_list = []
    right_list = []
    for p in range(block_total):
        for q in range(p + 1, block_total):
            left_list.append(p)
            right_list.append(q)
    return (np.array(left_list, dtype=np.int32), np.array(right_list, dtype=np.int32))


def make_kernel(u_part, v_part, block_total):
    u_cols = u_part.astype(jnp.float32).reshape(GRID, block_total, SBLK * SBLK).transpose(1, 2, 0)
    v_cols = v_part.astype(jnp.float32).reshape(GRID, block_total, SBLK * SBLK).transpose(1, 2, 0)
    product = u_cols[:, :, :, None] * v_cols[:, :, None, :]
    return product.reshape(block_total, SBLK * SBLK, GRID * GRID).astype(jnp.bfloat16)


def body(samples, taps, block_tile, tile_slots, kern_u, kern_v):
    station_count, frame_count, length = samples.shape
    channel_count = length // 2
    chan_size = lax.axis_size("chan")
    tm_size = lax.axis_size("tm")
    group_count = chan_size * tm_size
    group_width = channel_count // group_count
    tap_count = taps.shape[0]
    history = passed_along(samples[:, frame_count - (tap_count - 1) :], "tm", 1)
    padded = jnp.concatenate([history, samples], axis=1)
    filtered = jnp.zeros((station_count, frame_count, length), jnp.float32)
    for tap_index in range(tap_count):
        offset = tap_count - 1 - tap_index
        filtered = filtered + taps[tap_index] * padded[:, offset : offset + frame_count].astype(
            jnp.float32
        )
    rows_in = filtered.astype(jnp.bfloat16).reshape(station_count * frame_count, length)
    dft_scale = 1.0 / math.sqrt(length)
    block_cols = min(channel_count, 256)
    groups_per_block = block_cols // group_width
    positions = jnp.arange(length, dtype=jnp.int32)[:, None, None]
    pieces = []
    for column_block in range(channel_count // block_cols):
        channels = column_block * block_cols + jnp.arange(block_cols, dtype=jnp.int32).reshape(
            1, groups_per_block, group_width
        )
        phase_int = positions * channels % length
        phase_angle = phase_int.astype(jnp.float32) * (2.0 * math.pi / length)
        cosine = jnp.cos(phase_angle).astype(jnp.bfloat16)
        sine_neg = (-jnp.sin(phase_angle)).astype(jnp.bfloat16)
        dft_table = jnp.stack([cosine, sine_neg], axis=2).reshape(length, 2 * block_cols)
        spectrum = (
            lax.dot_general(
                dft_table, rows_in, (((0,), (1,)), ((), ())), preferred_element_type=jnp.float32
            )
            * dft_scale
        )
        pieces.append(
            spectrum.astype(jnp.bfloat16).reshape(
                groups_per_block, 2, group_width, station_count, frame_count
            )
        )
    spectra = jnp.concatenate(pieces, axis=0)
    stations = station_count * chan_size
    frames = frame_count * tm_size
    arranged = spectra.reshape(chan_size, tm_size, 2, group_width, station_count, frame_count)
    turned = lax.all_to_all(
        lax.all_to_all(arranged, "chan", split_axis=0, concat_axis=4, tiled=True),
        "tm",
        split_axis=1,
        concat_axis=5,
        tiled=True,
    )
    turned = turned.reshape(2, group_width, stations, frames)
    block_rows = stations // SBLK
    block_total = block_rows * (block_rows - 1) // 2
    vis_scale = 1.0 / math.sqrt(frames)
    swapped = jnp.stack([turned[1], -turned[0]], axis=0)
    real_part = (
        jnp.einsum("cgib,cgjb->gij", turned, turned, preferred_element_type=jnp.float32) * vis_scale
    )
    imag_part = (
        jnp.einsum("cgib,cgjb->gij", swapped, turned, preferred_element_type=jnp.float32)
        * vis_scale
    )
    left_idx, right_idx = block_pairs(block_rows)
    visibility = jnp.stack([real_part, imag_part], axis=1).reshape(
        group_width, 2, block_rows, SBLK, block_rows, SBLK
    )
    visibility = visibility[:, :, left_idx, :, right_idx, :]
    blocks = visibility.reshape(block_total, group_width, 2, SBLK * SBLK).astype(jnp.bfloat16)
    tile_count = tile_slots.shape[0]
    slot_ids = jnp.arange(tile_count, dtype=jnp.int32)
    tile_match = block_tile[:, None] == tile_slots[None, :]
    slot_of_block = jnp.sum(jnp.where(tile_match, slot_ids[None, :], 0), axis=1)
    kernel = make_kernel(kern_u, kern_v, block_total)
    per_block = jnp.einsum("mgce,mel->mgcl", blocks, kernel, preferred_element_type=jnp.float32)
    slot_hits = (slot_of_block[:, None] == slot_ids[None, :]).astype(jnp.float32)
    partial_value = jnp.einsum(
        "mgcl,ms->sgcl", per_block, slot_hits, precision=lax.Precision.HIGHEST
    )
    uv_grid = lax.all_to_all(partial_value, "tm", split_axis=0, concat_axis=1, tiled=True)
    return uv_grid


def solution(mesh):
    placed = (P("chan", "tm", None), P(), P(), P(), P(), P())
    return jax.shard_map(
        body, mesh=mesh, in_specs=placed, out_specs=P("tm", "chan", None, None), check_vma=False
    )
```

profile of v0, /device:TPU:1, one launch (start us, length us, event | category | flops | bytes accessed | tf_op | source)
XLA Modules:
  0.0 647.3 jit_solution(4451937538021533933)
XLA Ops:
  9.7 18.1 %cosine_convert_fusion.7 = (bf16[4096,16,1,16]{0,3,2,1:T(8,128)(2,1)S(1)}, bf16[4096,16,1,16]{0,3,2,1:T(8,128)(2,1)S(1)}) fusion(s32[16,16]{1,0:T(8,128)S(1)} %multiply_add_fusion), kind=kLoop, calls=%fused_computation.119 | loop fusion | flops 17825792 | bytes 4195328 | tf_op jit(solution)/shard_map/convert_element_type | solution.py:63
  27.7 18.1 %cosine_convert_fusion.6 = (bf16[4096,16,1,16]{0,3,2,1:T(8,128)(2,1)S(1)}, bf16[4096,16,1,16]{0,3,2,1:T(8,128)(2,1)S(1)}) fusion(s32[16,16]{1,0:T(8,128)S(1)} %fusion.84), kind=kLoop, calls=%fused_computation.115 | loop fusion | flops 17825792 | bytes 4195328 | tf_op jit(solution)/shard_map/convert_element_type | solution.py:63
  45.8 18.1 %cosine_convert_fusion.5 = (bf16[4096,16,1,16]{0,3,2,1:T(8,128)(2,1)S(1)}, bf16[4096,16,1,16]{0,3,2,1:T(8,128)(2,1)S(1)}) fusion(s32[16,16]{1,0:T(8,128)S(1)} %fusion.83), kind=kLoop, calls=%fused_computation.111 | loop fusion | flops 17825792 | bytes 4195328 | tf_op jit(solution)/shard_map/convert_element_type | solution.py:63
  63.9 18.1 %cosine_convert_fusion.4 = (bf16[4096,16,1,16]{0,3,2,1:T(8,128)(2,1)S(1)}, bf16[4096,16,1,16]{0,3,2,1:T(8,128)(2,1)S(1)}) fusion(s32[16,16]{1,0:T(8,128)S(1)} %fusion.82), kind=kLoop, calls=%fused_computation.107 | loop fusion | flops 17825792 | bytes 4195328 | tf_op jit(solution)/shard_map/convert_element_type | solution.py:63
  82.0 18.1 %cosine_convert_fusion.3 = (bf16[4096,16,1,16]{0,3,2,1:T(8,128)(2,1)S(1)}, bf16[4096,16,1,16]{0,3,2,1:T(8,128)(2,1)S(1)}) fusion(s32[16,16]{1,0:T(8,128)S(1)} %fusion.81), kind=kLoop, calls=%fused_computation.103 | loop fusion | flops 17825792 | bytes 4195328 | tf_op jit(solution)/shard_map/convert_element_type | solution.py:63
  100.0 18.1 %cosine_convert_fusion.2 = (bf16[4096,16,1,16]{0,3,2,1:T(8,128)(2,1)S(1)}, bf16[4096,16,1,16]{0,3,2,1:T(8,128)(2,1)S(1)}) fusion(s32[16,16]{1,0:T(8,128)S(1)} %fusion.80), kind=kLoop, calls=%fused_computation.99 | loop fusion | flops 17825792 | bytes 4195328 | tf_op jit(solution)/shard_map/convert_element_type | solution.py:63
  118.1 18.1 %cosine_convert_fusion.1 = (bf16[4096,16,1,16]{0,3,2,1:T(8,128)(2,1)S(1)}, bf16[4096,16,1,16]{0,3,2,1:T(8,128)(2,1)S(1)}) fusion(s32[16,16]{1,0:T(8,128)S(1)} %fusion.79), kind=kLoop, calls=%fused_computation.95 | loop fusion | flops 17825792 | bytes 4195328 | tf_op jit(solution)/shard_map/convert_element_type | solution.py:63
  136.2 19.0 %cosine_convert_fusion = (bf16[4096,16,1,16]{0,3,2,1:T(8,128)(2,1)S(1)}, bf16[4096,16,1,16]{0,3,2,1:T(8,128)(2,1)}) fusion(s32[16,16]{1,0:T(8,128)S(1)} %fusion.78), kind=kLoop, calls=%fused_computation.91 | loop fusion | flops 17825792 | bytes 4195328 | tf_op jit(solution)/shard_map/convert_element_type | solution.py:63
  178.3 23.2 %add_convert_fusion = bf16[16,24,4096]{2,1,0:T(8,128)(2,1)} fusion(bf16[16,24,4096]{2,1,0:T(8,128)(2,1)S(1)} %copy-done, bf16[16,15,4096]{2,1,0:T(8,128)(2,1)} %copy.81, f32[4096]{0:T(1024)S(1)} %bitcast.136, f32[4096]{0:T(1024)S(1)} %bitcast.137, f32[4096]{0:T(1024)S(1)} %bitcast.123, f32[4096]{0:T(1024)S(1)} %bitcast.124, f32[4096]{0:T(1024)S(1)} %bitcast.125, ...), kind=kLoop, calls=%fused_computation.52 | loop fusion | flops 146276352 | bytes 8519680 | tf_op jit(solution)/shard_map/convert_element_type | solution.py:51
  288.1 22.6 %reshape.779 = bf16[16,2,49152]{2,1,0:T(2,128)(2,1)S(1)} reshape(bf16[16,8,2,16,16,24]{5,4,3,2,1,0:T(8,128)(2,1)} %bitcast.96) | data formatting | bytes 6291456
  310.7 47.5 %all_to_all.51 = bf16[16,2,49152]{2,1,0:T(2,128)(2,1)} all-to-all(bf16[16,2,49152]{2,1,0:T(2,128)(2,1)S(1)} %reshape.779), channel_id=1, replica_groups=mesh['chan'=16,'tm'=8] {'chan'}, dimensions={0} | all-to-all | bytes 6291456 | tf_op jit(solution)/shard_map/all_to_all | solution.py:82
  358.2 25.0 %reshape.780 = bf16[16,8,2,16,16,24]{5,4,3,2,1,0:T(8,128)(2,1)} reshape(bf16[16,2,49152]{2,1,0:T(2,128)(2,1)} %all_to_all.51) | data formatting | bytes 6291456
  383.2 32.4 %copy.82 = bf16[1,8,2,16,16,16,24]{5,4,6,3,2,1,0:T(8,128)(2,1)} copy(bf16[1,8,2,16,16,16,24]{6,5,3,2,1,4,0:T(8,128)(2,1)} %bitcast.92) | data formatting | bytes 6291456 | tf_op jit(solution)/shard_map/all_to_all | solution.py:82
  415.6 30.1 %all_to_all.40 = bf16[1,8,2,16,256,24]{4,5,3,2,1,0:T(8,128)(2,1)} reshape(bf16[1,8,2,16,16,16,24]{5,4,6,3,2,1,0:T(8,128)(2,1)} %copy.82) | data formatting | bytes 6291456 | tf_op jit(solution)/shard_map/all_to_all | solution.py:82
  462.2 25.4 %all-to-all-done.1 = bf16[1,8,2,16,256,24]{4,5,3,2,0,1:T(8,128)(2,1)S(1)} async-done(((bf16[1,8,2,16,256,24]{4,5,3,2,0,1:T(8,128)(2,1)}), bf16[1,8,2,16,256,24]{4,5,3,2,0,1:T(8,128)(2,1)S(1)}, u32[]{:S(2)}, u32[]{:S(2)}) %all-to-all-start.1) | async-done | bytes 3145760 | tf_op jit(solution)/shard_map/all_to_all | solution.py:81
  492.8 17.4 %stack.63 = bf16[16,1,16,16,16,16]{5,4,3,2,0,1:T(8,128)(2,1)} reshape(bf16[16,256,256]{2,1,0:T(8,128)(2,1)} %bitcast_multiply_fusion) | data formatting | bytes 4194304 | tf_op jit(solution)/shard_map/stack | solution.py:101
  510.2 16.6 %copy.88 = bf16[16,1,16,16,16,16]{5,3,4,2,1,0:T(8,128)(2,1)} copy(bf16[16,1,16,16,16,16]{5,4,3,2,0,1:T(8,128)(2,1)} %stack.63) | data formatting | bytes 4194304 | tf_op jit(solution)/shard_map/stack | solution.py:101
  526.9 14.3 %stack.61 = bf16[16,1,16,16,16,16]{5,4,3,2,0,1:T(8,128)(2,1)} reshape(bf16[16,256,256]{2,1,0:T(8,128)(2,1)S(1)} %bitcast_multiply_fusion.1) | data formatting | bytes 4194304 | tf_op jit(solution)/shard_map/stack | solution.py:101
  541.2 16.6 %copy.87 = bf16[16,1,16,16,16,16]{5,3,4,2,1,0:T(8,128)(2,1)} copy(bf16[16,1,16,16,16,16]{5,4,3,2,0,1:T(8,128)(2,1)} %stack.61) | data formatting | bytes 4194304 | tf_op jit(solution)/shard_map/stack | solution.py:101
  557.8 22.7 %pad_maximum_fusion = bf16[16,2,16,16,16,16]{5,3,4,2,1,0:T(8,128)(2,1)} fusion(bf16[16,1,16,16,16,16]{5,3,4,2,1,0:T(8,128)(2,1)} %copy.88, bf16[16,1,16,16,16,16]{5,3,4,2,1,0:T(8,128)(2,1)} %copy.87), kind=kLoop, calls=%fused_computation.1 | loop fusion | flops 2097152 | bytes 8388608 | tf_op jit(solution)/shard_map/stack | solution.py:101
  580.5 12.2 %gather_fusion = bf16[120,16,2,16,16]{4,3,2,1,0:T(8,128)(2,1)} fusion(bf16[16,2,16,16,16,16]{5,3,4,2,1,0:T(8,128)(2,1)} %pad_maximum_fusion, s32[120]{0:T(128)S(1)} %copy-done.8), kind=kCustom, calls=%fused_computation | custom fusion | bytes 3933120 | tf_op jit(solution)/shard_map/gather | solution.py:104
  592.7 18.3 %copy.89 = bf16[120,16,2,16,16]{0,4,3,2,1:T(8,128)(2,1)S(1)} copy(bf16[120,16,2,16,16]{4,3,2,1,0:T(8,128)(2,1)} %gather_fusion) | data formatting | bytes 3932160 | tf_op jit(solution)/shard_map/gather | solution.py:104
  614.3 12.6 %fusion.91 = f32[120,16,2,256]{3,1,2,0:T(8,128)} fusion(bf16[120,16,2,256]{3,1,2,0:T(8,128)(2,1)} %copy.92, bf16[120,256,256,1]{1,2,3,0:T(8,128)(2,1)} %bitcast.93), kind=kOutput, calls=%fused_computation.193 | convolution fusion | flops 503316480 | bytes 21626880 | tf_op jit(solution)/shard_map/mgce,mel->mgcl/dot_general | solution.py:111
  633.2 12.6 %all_to_all.52 = f32[16,16,2,256]{3,2,1,0:T(2,128)S(1)} all-to-all(f32[16,16,2,256]{3,2,1,0:T(2,128)S(1)} %copy.95), channel_id=1, replica_groups=mesh['chan'=16,'tm'=8] {'tm'}, dimensions={0} | all-to-all | bytes 1048576 | tf_op jit(solution)/shard_map/all_to_all | solution.py:116
  (88 shorter events, 151.3 us)
Async XLA Ops:
  4.6 169.6 %collective-permute-start = (bf16[16,15,4096]{2,0,1:T(8,128)(2,1)}, bf16[16,15,4096]{2,0,1:T(8,128)(2,1)}, u32[]{:S(2)}, u32[]{:S(2)}) collective-permute-start(bf16[16,15,4096]{2,0,1:T(8,128)(2,1)} %copy.103), channel_id=1, source_target_pairs={{0,1},{1,2},{2,3},{3,4},{4,5},{5,6},{6,7},{8,9},{9,10},{10,11},{11... | collective-permute-start | bytes 5898248 | tf_op jit(solution)/shard_map/ppermute | solution.py:15
  169.3 2.3 copy-start.7
  171.6 2.4 copy-start.10
  174.0 4.4 copy-start
  209.8 2.9 copy-start.9
  275.6 2.2 copy-start.1
  275.6 3.9 copy-start.2
  277.8 3.4 copy-start.3
  279.5 3.5 copy-start.4
  281.2 3.5 copy-start.5
  283.0 3.4 copy-start.6
  445.7 42.0 %all-to-all-start.1 = ((bf16[1,8,2,16,256,24]{4,5,3,2,0,1:T(8,128)(2,1)}), bf16[1,8,2,16,256,24]{4,5,3,2,0,1:T(8,128)(2,1)S(1)}, u32[]{:S(2)}, u32[]{:S(2)}) async-start(bf16[1,8,2,16,256,24]{4,5,3,2,0,1:T(8,128)(2,1)} %bitcast.97), calls=%async_computation.1 | async-start | bytes 6291456 | tf_op jit(solution)/shard_map/all_to_all | solution.py:81
  450.1 2.7 copy-start.11
  450.1 2.7 copy-start.12
  557.8 22.7 %copy-start.8 = (s32[120]{0:T(128)S(1)}, s32[120]{0:T(128)}, u32[]{:S(2)}) copy-start(s32[120]{0:T(128)} %constant.106) | copy-start | bytes 1444
where the time goes:
time: 658 us; the launch traced here: 647 us
  local copies, waits for them, and re-layouts  264 us (40%)
  other arithmetic  222 us (34%)
  matrix products  65.5 us (10%)
  blocking collectives  60.1 us (9%)
  waiting for transfers between devices  25.4 us (4%)
  starting transfers between devices  9.37 us (1%)
    convert_element_type x8, other arithmetic, body(): cosine = jnp.cos(phase_angle).astype(jnp.bfloat16)  145 us
    another operation x4, local copies, waits for them, and re-layouts, body(): jnp.stack([real_part, imag_part], axis=1)  65 us
    unnamed x36, local copies, waits for them, and re-layouts  63.9 us
    all_to_all x2, local copies, waits for them, and re-layouts, body(): lax.all_to_all(arranged, 'chan', split_axis=0, concat_axis=4, tiled=True)  62.5 us
    all_to_all x1, blocking collectives, body(): lax.all_to_all(arranged, 'chan', split_axis=0, concat_axis=4, tiled=True)  47.5 us
    dot_general x8, matrix products, body(): lax.dot_general(dft_table, rows_in, (((0,), (1,)), ((), ())), preferred_e...  42.9 us
    gather x2, local copies, waits for them, and re-layouts, body(): visibility = visibility[:, :, left_idx, :, right_idx, :]  30.6 us
    reshape x8, local copies, waits for them, and re-layouts, body(): spectrum.astype(jnp.bfloat16)  28.2 us
  transfers between devices with their start and end apart: 2, of which 1 were waited for; matrix products, arithmetic and copies ran while one was open for 27% of the time, Pallas kernels for 0%

commit v1 on v0

--- a/solution.py
+++ b/solution.py
@@ -78,12 +78,20 @@
     stations = station_count * chan_size
     frames = frame_count * tm_size
     arranged = spectra.reshape(chan_size, tm_size, 2, group_width, station_count, frame_count)
-    turned = lax.all_to_all(
-        lax.all_to_all(arranged, "chan", split_axis=0, concat_axis=4, tiled=True),
-        "tm",
-        split_axis=1,
-        concat_axis=5,
-        tiled=True,
+    turned = jnp.concatenate(
+        jax.lax.all_to_all(
+            jnp.stack(
+                jnp.split(
+                    lax.all_to_all(arranged, "chan", split_axis=0, concat_axis=4, tiled=True),
+                    jax.lax.psum(1, axis_name="tm"),
+                    axis=1,
+                )
+            ),
+            axis_name="tm",
+            split_axis=0,
+            concat_axis=0,
+        ),
+        axis=5,
     )
     turned = turned.reshape(2, group_width, stations, frames)
     block_rows = stations // SBLK

time: 658 us -> 663 us (level)
    unnamed x36 -> x43, local copies, waits for them, and re-layouts: 63.9 us -> 69.3 us
where the time goes in v1:
time: 663 us; the launch traced here: 652 us
  local copies, waits for them, and re-layouts  269 us (41%)
  other arithmetic  222 us (33%)
  matrix products  65.5 us (10%)
  blocking collectives  60.1 us (9%)
  waiting for transfers between devices  25.4 us (4%)
  starting transfers between devices  9.37 us (1%)
    convert_element_type x8, other arithmetic, body(): cosine = jnp.cos(phase_angle).astype(jnp.bfloat16)  145 us
    unnamed x43, local copies, waits for them, and re-layouts  69.3 us
    another operation x4, local copies, waits for them, and re-layouts, body(): jnp.stack([real_part, imag_part], axis=1)  65 us
    all_to_all x2, local copies, waits for them, and re-layouts, body(): lax.all_to_all(arranged, 'chan', split_axis=0, concat_axis=4, tiled=True)  60.9 us
    all_to_all x1, blocking collectives, body(): lax.all_to_all(arranged, 'chan', split_axis=0, concat_axis=4, tiled=True)  47.5 us
    dot_general x8, matrix products, body(): lax.dot_general(dft_table, rows_in, (((0,), (1,)), ((), ())), preferred_e...  42.9 us
    gather x2, local copies, waits for them, and re-layouts, body(): visibility = visibility[:, :, left_idx, :, right_idx, :]  30.6 us
    reshape x8, local copies, waits for them, and re-layouts, body(): spectrum.astype(jnp.bfloat16)  28.2 us
  transfers between devices with their start and end apart: 2, of which 1 were waited for; matrix products, arithmetic and copies ran while one was open for 27% of the time, Pallas kernels for 0%

profile of v1, /device:TPU:1, one launch (start us, length us, event | category | flops | bytes accessed | tf_op | source)
XLA Modules:
  0.0 651.9 jit_solution(15957559578955189802)
XLA Ops:
  9.7 18.1 %cosine_convert_fusion.7 = (bf16[4096,16,1,16]{0,3,2,1:T(8,128)(2,1)S(1)}, bf16[4096,16,1,16]{0,3,2,1:T(8,128)(2,1)S(1)}) fusion(s32[16,16]{1,0:T(8,128)S(1)} %multiply_add_fusion), kind=kLoop, calls=%fused_computation.119 | loop fusion | flops 17825792 | bytes 4195328 | tf_op jit(solution)/shard_map/convert_element_type | solution.py:63
  27.7 18.1 %cosine_convert_fusion.6 = (bf16[4096,16,1,16]{0,3,2,1:T(8,128)(2,1)S(1)}, bf16[4096,16,1,16]{0,3,2,1:T(8,128)(2,1)S(1)}) fusion(s32[16,16]{1,0:T(8,128)S(1)} %fusion.92), kind=kLoop, calls=%fused_computation.115 | loop fusion | flops 17825792 | bytes 4195328 | tf_op jit(solution)/shard_map/convert_element_type | solution.py:63
  45.8 18.1 %cosine_convert_fusion.5 = (bf16[4096,16,1,16]{0,3,2,1:T(8,128)(2,1)S(1)}, bf16[4096,16,1,16]{0,3,2,1:T(8,128)(2,1)S(1)}) fusion(s32[16,16]{1,0:T(8,128)S(1)} %fusion.91), kind=kLoop, calls=%fused_computation.111 | loop fusion | flops 17825792 | bytes 4195328 | tf_op jit(solution)/shard_map/convert_element_type | solution.py:63
  63.9 18.1 %cosine_convert_fusion.4 = (bf16[4096,16,1,16]{0,3,2,1:T(8,128)(2,1)S(1)}, bf16[4096,16,1,16]{0,3,2,1:T(8,128)(2,1)S(1)}) fusion(s32[16,16]{1,0:T(8,128)S(1)} %fusion.90), kind=kLoop, calls=%fused_computation.107 | loop fusion | flops 17825792 | bytes 4195328 | tf_op jit(solution)/shard_map/convert_element_type | solution.py:63
  82.0 18.1 %cosine_convert_fusion.3 = (bf16[4096,16,1,16]{0,3,2,1:T(8,128)(2,1)S(1)}, bf16[4096,16,1,16]{0,3,2,1:T(8,128)(2,1)S(1)}) fusion(s32[16,16]{1,0:T(8,128)S(1)} %fusion.89), kind=kLoop, calls=%fused_computation.103 | loop fusion | flops 17825792 | bytes 4195328 | tf_op jit(solution)/shard_map/convert_element_type | solution.py:63
  100.0 18.1 %cosine_convert_fusion.2 = (bf16[4096,16,1,16]{0,3,2,1:T(8,128)(2,1)S(1)}, bf16[4096,16,1,16]{0,3,2,1:T(8,128)(2,1)S(1)}) fusion(s32[16,16]{1,0:T(8,128)S(1)} %fusion.88), kind=kLoop, calls=%fused_computation.99 | loop fusion | flops 17825792 | bytes 4195328 | tf_op jit(solution)/shard_map/convert_element_type | solution.py:63
  118.1 18.1 %cosine_convert_fusion.1 = (bf16[4096,16,1,16]{0,3,2,1:T(8,128)(2,1)S(1)}, bf16[4096,16,1,16]{0,3,2,1:T(8,128)(2,1)S(1)}) fusion(s32[16,16]{1,0:T(8,128)S(1)} %fusion.87), kind=kLoop, calls=%fused_computation.95 | loop fusion | flops 17825792 | bytes 4195328 | tf_op jit(solution)/shard_map/convert_element_type | solution.py:63
  136.2 19.0 %cosine_convert_fusion = (bf16[4096,16,1,16]{0,3,2,1:T(8,128)(2,1)S(1)}, bf16[4096,16,1,16]{0,3,2,1:T(8,128)(2,1)}) fusion(s32[16,16]{1,0:T(8,128)S(1)} %fusion.86), kind=kLoop, calls=%fused_computation.91 | loop fusion | flops 17825792 | bytes 4195328 | tf_op jit(solution)/shard_map/convert_element_type | solution.py:63
  178.3 23.2 %add_convert_fusion = bf16[16,24,4096]{2,1,0:T(8,128)(2,1)} fusion(bf16[16,24,4096]{2,1,0:T(8,128)(2,1)S(1)} %copy-done, bf16[16,15,4096]{2,1,0:T(8,128)(2,1)} %copy.86, f32[4096]{0:T(1024)S(1)} %bitcast.164, f32[4096]{0:T(1024)S(1)} %bitcast.165, f32[4096]{0:T(1024)S(1)} %bitcast.151, f32[4096]{0:T(1024)S(1)} %bitcast.152, f32[4096]{0:T(1024)S(1)} %bitcast.153, ...), kind=kLoop, calls=%fused_computation.52 | loop fusion | flops 146276352 | bytes 8519680 | tf_op jit(solution)/shard_map/convert_element_type | solution.py:51
  288.1 22.6 %reshape.778 = bf16[16,2,49152]{2,1,0:T(2,128)(2,1)S(1)} reshape(bf16[16,8,2,16,16,24]{5,4,3,2,1,0:T(8,128)(2,1)} %bitcast.125) | data formatting | bytes 6291456
  310.7 47.5 %all_to_all.41 = bf16[16,2,49152]{2,1,0:T(2,128)(2,1)} all-to-all(bf16[16,2,49152]{2,1,0:T(2,128)(2,1)S(1)} %reshape.778), channel_id=1, replica_groups=mesh['chan'=16,'tm'=8] {'chan'}, dimensions={0} | all-to-all | bytes 6291456 | tf_op jit(solution)/shard_map/all_to_all | solution.py:85
  358.2 25.0 %reshape.779 = bf16[16,8,2,16,16,24]{5,4,3,2,1,0:T(8,128)(2,1)} reshape(bf16[16,2,49152]{2,1,0:T(2,128)(2,1)} %all_to_all.41) | data formatting | bytes 6291456
  383.2 32.4 %copy.87 = bf16[1,8,2,16,16,16,24]{5,4,6,3,2,1,0:T(8,128)(2,1)} copy(bf16[1,8,2,16,16,16,24]{6,5,3,2,1,4,0:T(8,128)(2,1)} %bitcast.121) | data formatting | bytes 6291456 | tf_op jit(solution)/shard_map/all_to_all | solution.py:85
  415.6 28.5 %all_to_all.32 = bf16[1,8,2,16,256,24]{4,5,3,2,1,0:T(8,128)(2,1)S(1)} reshape(bf16[1,8,2,16,16,16,24]{5,4,6,3,2,1,0:T(8,128)(2,1)} %copy.87) | data formatting | bytes 6291456 | tf_op jit(solution)/shard_map/all_to_all | solution.py:85
  466.9 25.4 %all-to-all-done.1 = bf16[8,1,1,2,16,256,24]{5,6,4,3,2,1,0:T(8,128)(2,1)S(1)} async-done(((bf16[8,1,1,2,16,256,24]{5,6,4,3,2,1,0:T(8,128)(2,1)}), bf16[8,1,1,2,16,256,24]{5,6,4,3,2,1,0:T(8,128)(2,1)S(1)}, u32[]{:S(2)}, u32[]{:S(2)}) %all-to-all-start.1) | async-done | bytes 3145760 | tf_op jit(solution)/shard_map/all_to_all | solution.py:82
  497.5 17.4 %stack.99 = bf16[16,1,16,16,16,16]{5,4,3,2,0,1:T(8,128)(2,1)} reshape(bf16[16,256,256]{2,1,0:T(8,128)(2,1)} %bitcast_multiply_fusion) | data formatting | bytes 4194304 | tf_op jit(solution)/shard_map/stack | solution.py:109
  514.9 16.6 %copy.92 = bf16[16,1,16,16,16,16]{5,3,4,2,1,0:T(8,128)(2,1)} copy(bf16[16,1,16,16,16,16]{5,4,3,2,0,1:T(8,128)(2,1)} %stack.99) | data formatting | bytes 4194304 | tf_op jit(solution)/shard_map/stack | solution.py:109
  531.6 14.3 %stack.97 = bf16[16,1,16,16,16,16]{5,4,3,2,0,1:T(8,128)(2,1)} reshape(bf16[16,256,256]{2,1,0:T(8,128)(2,1)S(1)} %bitcast_multiply_fusion.1) | data formatting | bytes 4194304 | tf_op jit(solution)/shard_map/stack | solution.py:109
  545.9 16.6 %copy.91 = bf16[16,1,16,16,16,16]{5,3,4,2,1,0:T(8,128)(2,1)} copy(bf16[16,1,16,16,16,16]{5,4,3,2,0,1:T(8,128)(2,1)} %stack.97) | data formatting | bytes 4194304 | tf_op jit(solution)/shard_map/stack | solution.py:109
  562.5 22.7 %pad_maximum_fusion = bf16[16,2,16,16,16,16]{5,3,4,2,1,0:T(8,128)(2,1)} fusion(bf16[16,1,16,16,16,16]{5,3,4,2,1,0:T(8,128)(2,1)} %copy.92, bf16[16,1,16,16,16,16]{5,3,4,2,1,0:T(8,128)(2,1)} %copy.91), kind=kLoop, calls=%fused_computation.1 | loop fusion | flops 2097152 | bytes 8388608 | tf_op jit(solution)/shard_map/stack | solution.py:109
  585.2 12.2 %gather_fusion = bf16[120,16,2,16,16]{4,3,2,1,0:T(8,128)(2,1)} fusion(bf16[16,2,16,16,16,16]{5,3,4,2,1,0:T(8,128)(2,1)} %pad_maximum_fusion, s32[120]{0:T(128)S(1)} %copy-done.8), kind=kCustom, calls=%fused_computation | custom fusion | bytes 3933120 | tf_op jit(solution)/shard_map/gather | solution.py:112
  597.4 18.3 %copy.93 = bf16[120,16,2,16,16]{0,4,3,2,1:T(8,128)(2,1)S(1)} copy(bf16[120,16,2,16,16]{4,3,2,1,0:T(8,128)(2,1)} %gather_fusion) | data formatting | bytes 3932160 | tf_op jit(solution)/shard_map/gather | solution.py:112
  619.0 12.6 %fusion.99 = f32[120,16,2,256]{3,1,2,0:T(8,128)} fusion(bf16[120,16,2,256]{3,1,2,0:T(8,128)(2,1)} %copy.96, bf16[120,256,256,1]{1,2,3,0:T(8,128)(2,1)} %bitcast.122), kind=kOutput, calls=%fused_computation.209 | convolution fusion | flops 503316480 | bytes 21626880 | tf_op jit(solution)/shard_map/mgce,mel->mgcl/dot_general | solution.py:119
  637.8 12.6 %all_to_all.42 = f32[16,16,2,256]{3,2,1,0:T(2,128)S(1)} all-to-all(f32[16,16,2,256]{3,2,1,0:T(2,128)S(1)} %copy.99), channel_id=1, replica_groups=mesh['chan'=16,'tm'=8] {'tm'}, dimensions={0} | all-to-all | bytes 1048576 | tf_op jit(solution)/shard_map/all_to_all | solution.py:124
  (96 shorter events, 157.5 us)
Async XLA Ops:
  4.6 169.6 %collective-permute-start = (bf16[16,15,4096]{2,0,1:T(8,128)(2,1)}, bf16[16,15,4096]{2,0,1:T(8,128)(2,1)}, u32[]{:S(2)}, u32[]{:S(2)}) collective-permute-start(bf16[16,15,4096]{2,0,1:T(8,128)(2,1)} %copy.107), channel_id=1, source_target_pairs={{0,1},{1,2},{2,3},{3,4},{4,5},{5,6},{6,7},{8,9},{9,10},{10,11},{11... | collective-permute-start | bytes 5898248 | tf_op jit(solution)/shard_map/ppermute | solution.py:15
  169.3 2.3 copy-start.7
  171.6 2.4 copy-start.10
  174.0 4.4 copy-start
  209.8 2.9 copy-start.9
  275.6 2.2 copy-start.1
  275.6 3.9 copy-start.2
  277.8 3.4 copy-start.3
  279.5 3.5 copy-start.4
  281.2 3.5 copy-start.5
  283.0 3.4 copy-start.6
  450.4 42.0 %all-to-all-start.1 = ((bf16[8,1,1,2,16,256,24]{5,6,4,3,2,1,0:T(8,128)(2,1)}), bf16[8,1,1,2,16,256,24]{5,6,4,3,2,1,0:T(8,128)(2,1)S(1)}, u32[]{:S(2)}, u32[]{:S(2)}) async-start(bf16[8,1,1,2,16,256,24]{5,6,4,3,2,1,0:T(8,128)(2,1)} %fusion.78), calls=%async_computation.1 | async-start | bytes 6291456 | tf_op jit(solution)/shard_map/all_to_all | solution.py:82
  454.8 2.7 copy-start.11
  454.8 2.7 copy-start.12
  562.5 22.7 %copy-start.8 = (s32[120]{0:T(128)S(1)}, s32[120]{0:T(128)}, u32[]{:S(2)}) copy-start(s32[120]{0:T(128)} %constant.106) | copy-start | bytes 1444
